TPU v7x, 32 devices: a whole 2x2x4 slice. The times are simulated.
32 devices in a mesh: energy: 4 (over y, core), layer: 8 (over z, x).
Axes of the slice: x: 2, y: 2, z: 4, core: 2. Of those that a mesh axis runs over, the one named last changes fastest.
Arguments:
- correlations: bfloat16 [32, 8, 4, 256, 256], P(('energy', 'layer')), may hold values from -6 to 6
- retarded: bfloat16 [32, 8, 2, 256, 256], P(('energy', 'layer')), may hold values from -0.15625 to 0.15625
- coupling: bfloat16 [8, 256, 256], P('layer'), may hold values from -0.375 to 0.375
- phonon_shifts: int32 [4], replicated, may hold values from 1 to 4, as said below
- phonon_coupling: float32 [4], replicated, may hold values from 0.3 to 1.2
- layer_orbitals: int32 [8], P('layer'), may hold values from 128 to 256, as said below
Outputs:
- left_correlations: bfloat16 [32, 8, 4, 256, 256], P('energy', 'layer')
Inputs may be any that keep to these rules, and one draw needn't show every extreme that they name: `phonon_shifts`: one of the offsets equals 4. `layer_orbitals`: some layer has all 256 orbitals live.
All inputs are finite; a program needn't handle non-finite values.
Results may differ from a plain program's by a relative error of at most 0.025.
Values may be sent and summed in bfloat16 or wider, within the bound.
A program may use at most 128 MiB of HBM per device.

v0:
```python
import jax
import jax.numpy as jnp
from jax import lax
from jax.sharding import PartitionSpec as P

MODES = 4
SHIFT_MAX = 4


bose_ratio = 0.5


def with_halo(block, sides, width):
    for axis, dim in sides:
        count = lax.axis_size(axis)
        forward = [(i, i + 1) for i in range(count - 1)]
        backward = [(target, source) for source, target in forward]
        low = lax.ppermute(
            lax.slice_in_dim(block, block.shape[dim] - width, None, axis=dim), axis, forward
        )
        high = lax.ppermute(lax.slice_in_dim(block, 0, width, axis=dim), axis, backward)
        block = jnp.concatenate([low, block, high], axis=dim)
    return block


def mode_weights(shift_value):
    occupation = 1.0 / (jnp.exp(bose_ratio * shift_value.astype(jnp.float32)) - 1.0)
    lower_weight = jnp.stack([occupation, occupation, occupation + 1.0, occupation + 1.0])
    upper_weight = jnp.stack([occupation + 1.0, occupation + 1.0, occupation, occupation])
    return (lower_weight, upper_weight)


def left_product(matrix, stacked_block):
    return jnp.einsum(
        "...ab,...kbc->...kac", matrix, stacked_block, preferred_element_type=jnp.float32
    )


def right_product(stacked_block, matrix):
    return jnp.einsum(
        "...kab,...cb->...kac", stacked_block, matrix, preferred_element_type=jnp.float32
    )


def advance(previous, sigma_block, green_block, coupling_block):
    halfway = jnp.einsum(
        "...kab,cb->...kac", previous, coupling_block, preferred_element_type=jnp.float32
    ).astype(jnp.bfloat16)
    spread = jnp.einsum(
        "ab,...kbc->...kac", coupling_block, halfway, preferred_element_type=jnp.float32
    )
    source = (sigma_block.astype(jnp.float32) + spread).astype(jnp.bfloat16)
    green_real = green_block[..., 0, :, :]
    green_imag = green_block[..., 1, :, :]
    source_real = source[..., 0::2, :, :]
    source_imag = source[..., 1::2, :, :]
    inner_real = (
        left_product(green_real, source_real) - left_product(green_imag, source_imag)
    ).astype(jnp.bfloat16)
    inner_imag = (
        left_product(green_real, source_imag) + left_product(green_imag, source_real)
    ).astype(jnp.bfloat16)
    outer_real = right_product(inner_real, green_real) + right_product(inner_imag, green_imag)
    outer_imag = right_product(inner_imag, green_real) - right_product(inner_real, green_imag)
    stacked = jnp.stack([outer_real, outer_imag], axis=-3)
    return stacked.reshape(stacked.shape[:-4] + (4,) + stacked.shape[-2:]).astype(jnp.bfloat16)


def body(correlations, retarded, coupling, phonon_shifts, phonon_coupling, layer_orbitals):
    regrouped = lax.all_to_all(correlations, "layer", split_axis=1, concat_axis=0, tiled=True)
    energies_here = regrouped.shape[0]
    orbital_count = regrouped.shape[-1]
    padded = with_halo(regrouped, (("energy", 0),), SHIFT_MAX)
    accumulated = jnp.zeros(regrouped.shape, jnp.float32)
    for mode_index in range(MODES):
        shift_value = phonon_shifts[mode_index]
        lower_weight, upper_weight = mode_weights(shift_value)
        lower_block = lax.dynamic_slice_in_dim(padded, SHIFT_MAX - shift_value, energies_here, 0)
        upper_block = lax.dynamic_slice_in_dim(padded, SHIFT_MAX + shift_value, energies_here, 0)
        accumulated = accumulated + phonon_coupling[mode_index] * (
            lower_weight[:, None, None] * lower_block.astype(jnp.float32)
            + upper_weight[:, None, None] * upper_block.astype(jnp.float32)
        )
    orbital_index = jnp.arange(orbital_count, dtype=jnp.int32)
    live_count = layer_orbitals[:, None, None, None]
    live_mask = (orbital_index[:, None] < live_count) & (orbital_index[None, :] < live_count)
    sigma_blocks = jnp.where(live_mask, accumulated, 0.0).astype(jnp.bfloat16)
    returned = lax.all_to_all(sigma_blocks, "layer", split_axis=0, concat_axis=1, tiled=True)
    couplings = lax.all_gather(coupling, "layer", axis=0, tiled=True)
    layer_total = returned.shape[1]

    def layer_step(layer_index, state):
        previous, finished = state
        current = advance(
            previous,
            lax.dynamic_index_in_dim(returned, layer_index, 1, keepdims=False),
            lax.dynamic_index_in_dim(retarded, layer_index, 1, keepdims=False),
            lax.dynamic_index_in_dim(couplings, layer_index, 0, keepdims=False),
        )
        finished = lax.dynamic_update_index_in_dim(finished, current, layer_index, 1)
        return (current, finished)

    _, finished = lax.fori_loop(
        0, layer_total, layer_step, (correlations[:, 0], jnp.zeros_like(correlations))
    )
    return lax.all_to_all(finished, "layer", split_axis=1, concat_axis=0, tiled=True)


def solution(mesh):
    return jax.shard_map(
        body,
        mesh=mesh,
        in_specs=(
            P(("energy", "layer"), None, None, None, None),
            P(("energy", "layer"), None, None, None, None),
            P("layer", None, None),
            P(),
            P(),
            P("layer"),
        ),
        out_specs=P("energy", "layer", None, None, None),
        check_vma=False,
    )
```

profile of v0, /device:TPU:27, one launch (start us, length us, event | category | flops | bytes accessed | tf_op | source)
XLA Modules:
  0.0 410.9 jit_solution(7461025328125969280)
XLA Ops:
  6.5 6.4 %copy.25 = bf16[1,8,4,256,256]{3,4,2,0,1:T(8,128)(2,1)} copy(bf16[1,8,4,256,256]{4,3,2,1,0:T(8,128)(2,1)} %param.8) | data formatting | bytes 8388608 | tf_op args[0]
  13.0 96.5 %all_to_all.39 = bf16[1,8,4,256,256]{3,4,2,0,1:T(8,128)(2,1)S(1)} all-to-all(bf16[1,8,4,256,256]{3,4,2,0,1:T(8,128)(2,1)} %copy.25), channel_id=1, replica_groups=mesh['energy'=4,'layer'=8] {'layer'}, dimensions={1} | all-to-all | bytes 8388608 | tf_op jit(solution)/shard_map/all_to_all | solution.py:70
  109.7 4.1 collective-permute-start
  113.7 1.5 slice_bitcast_fusion.10
  115.2 1.9 collective-permute-start.1
  131.7 5.0 %collective-permute-done = bf16[4,1,4,256,256]{3,4,2,0,1:T(8,128)(2,1)} collective-permute-done((bf16[4,1,4,256,256]{3,4,2,0,1:T(8,128)(2,1)S(1)}, bf16[4,1,4,256,256]{3,4,2,0,1:T(8,128)(2,1)}, u32[]{:S(2)}, u32[]{:S(2)}) %collective-permute-start) | collective-permute-done | bytes 2097184 | tf_op jit(solution)/shard_map/ppermute | solution.py:18
  136.7 6.2 %collective-permute-done.1 = bf16[4,1,4,256,256]{3,4,2,0,1:T(8,128)(2,1)} collective-permute-done((bf16[4,1,4,256,256]{3,4,2,0,1:T(8,128)(2,1)}, bf16[4,1,4,256,256]{3,4,2,0,1:T(8,128)(2,1)}, u32[]{:S(2)}, u32[]{:S(2)}) %collective-permute-start.1) | collective-permute-done | bytes 2097184 | tf_op jit(solution)/shard_map/ppermute | solution.py:21
  142.9 4.3 %pad_maximum_fusion = bf16[16,1,4,256,256]{3,4,2,0,1:T(8,128)(2,1)S(1)} fusion(bf16[4,1,4,256,256]{3,4,2,0,1:T(8,128)(2,1)} %collective-permute-done.1, bf16[8,1,4,256,256]{3,4,2,0,1:T(8,128)(2,1)} %bitcast.174, bf16[4,1,4,256,256]{3,4,2,0,1:T(8,128)(2,1)} %collective-permute-done), kind=kLoop, calls=%fused_computation.36 | loop fusion | flops 8388608 | bytes 16777216 | tf_op jit(solution)/shard_map/concatenate | solution.py:22
  147.2 11.6 %fusion.29 = bf16[8,1,4,256,256]{3,4,2,1,0:T(8,128)(2,1)} fusion(bf16[16,1,4,256,256]{3,4,2,0,1:T(8,128)(2,1)S(1)} %pad_maximum_fusion, s32[]{:T(128)S(6)} %select_n.47, f32[4]{0:T(128)S(1)} %get-tuple-element.136, s32[]{:T(128)S(6)} %select_n.46, f32[4]{0:T(128)S(1)} %get-tuple-element.135, f32[]{:T(128)} %bitcast.51, s32[]{:T(128)S(6)} %select_n.45, ...), kind=kLoop, calls=%fused_computation.38 | loop fusion | flops 60817408 | bytes 37814448 | tf_op jit(solution)/shard_map/convert_element_type | solution.py:87
  158.8 6.6 %all-to-all-start.1 = ((bf16[8,1,4,256,256]{3,4,2,1,0:T(8,128)(2,1)}), bf16[8,1,4,256,256]{3,4,2,1,0:T(8,128)(2,1)}, u32[]{:S(2)}, u32[]{:S(2)}) async-start(bf16[8,1,4,256,256]{3,4,2,1,0:T(8,128)(2,1)} %fusion.29), calls=%async_computation.1 | async-start | bytes 8388608 | tf_op jit(solution)/shard_map/all_to_all | solution.py:88
  166.1 1.1 slice_bitcast_fusion.12
  167.2 61.9 %all-gather.2.cloned.1.call-done = bf16[8,256,256]{2,1,0:T(8,128)(2,1)} async-done(((bf16[1,256,256]{2,1,0:T(8,128)(2,1)}), bf16[8,256,256]{2,1,0:T(8,128)(2,1)}) %all-gather.2.cloned.1.call-update) | async-done | bytes 1048592 | tf_op jit(solution)/shard_map/all_gather | solution.py:89
  229.1 28.6 %all-to-all-done.1 = bf16[8,1,4,256,256]{3,4,2,1,0:T(8,128)(2,1)} async-done(((bf16[8,1,4,256,256]{3,4,2,1,0:T(8,128)(2,1)}), bf16[8,1,4,256,256]{3,4,2,1,0:T(8,128)(2,1)}, u32[]{:S(2)}, u32[]{:S(2)}) %all-to-all-start.1) | async-done | bytes 4194336 | tf_op jit(solution)/shard_map/all_to_all | solution.py:88
  257.7 46.5 %while.15 = (s32[]{:T(128)}, bf16[1,4,256,256]{3,2,1,0:T(8,128)(2,1)S(1)}, bf16[1,8,4,256,256]{4,3,2,1,0:T(8,128)(2,1)}, bf16[1,8,4,256,256]{3,4,2,1,0:T(8,128)(...) while((s32[]{:T(128)}, bf16[1,4,256,256]{3,2,1,0:T(8,128)(2,1)S(1)}, ...), condition=%wide.region_1.2_spmd, body=%wide.region_0.1_spmd.sunk | while | flops 807665664 | bytes 13895761 | solution.py:103
  258.7 1.7 fusion.67
  264.5 1.7 fusion.67
  270.3 1.7 fusion.67
  276.1 1.7 fusion.67
  281.9 1.7 fusion.67
  287.7 1.7 fusion.67
  293.6 1.7 fusion.67
  299.4 1.7 fusion.67
  304.2 97.8 %all_to_all.40 = bf16[1,8,4,256,256]{4,3,2,0,1:T(8,128)(2,1)S(1)} all-to-all(bf16[1,8,4,256,256]{4,3,2,0,1:T(8,128)(2,1)} %bitcast.58), channel_id=1, replica_groups=mesh['energy'=4,'layer'=8] {'layer'}, dimensions={1} | all-to-all | bytes 8388608 | tf_op jit(solution)/shard_map/all_to_all | solution.py:106
  402.0 2.0 copy.49
  (114 shorter events, 34.8 us)
Async XLA Ops:
  13.0 104.2 %copy-start.1 = (s32[4]{0:T(128)S(1)}, s32[4]{0:T(128)}, u32[]{:S(2)}) copy-start(s32[4]{0:T(128)} %param.11) | copy-start | bytes 52
  13.0 118.0 %copy-start.2 = (f32[4]{0:T(128)S(1)}, f32[4]{0:T(128)}, u32[]{:S(2)}) copy-start(f32[4]{0:T(128)} %param.12) | copy-start | bytes 52
  109.5 4.2 %copy-start = (bf16[1,8,4,256,256]{3,4,2,0,1:T(8,128)(2,1)}, bf16[1,8,4,256,256]{3,4,2,0,1:T(8,128)(2,1)S(1)}, u32[]{:S(2)}) copy-start(bf16[1,8,4,256,256]{3,4,2,0,1:T(8,128)(2,1)S(1)} %all_to_all.39) | copy-start | bytes 12582916
  109.7 27.0 %collective-permute-start = (bf16[4,1,4,256,256]{3,4,2,0,1:T(8,128)(2,1)S(1)}, bf16[4,1,4,256,256]{3,4,2,0,1:T(8,128)(2,1)}, u32[]{:S(2)}, u32[]{:S(2)}) collective-permute-start(bf16[4,1,4,256,256]{3,4,2,0,1:T(8,128)(2,1)S(1)} %slice_bitcast_fusion.11), channel_id=1, source_target_pairs={{0,8},{8,16},{16,24},{1,9},{9,17},{17,25},{2,10},{10,18},{18,26},{... | collective-permute-start | bytes 6291464 | tf_op jit(solution)/shard_map/ppermute | solution.py:18
  115.2 27.7 %collective-permute-start.1 = (bf16[4,1,4,256,256]{3,4,2,0,1:T(8,128)(2,1)}, bf16[4,1,4,256,256]{3,4,2,0,1:T(8,128)(2,1)}, u32[]{:S(2)}, u32[]{:S(2)}) collective-permute-start(bf16[4,1,4,256,256]{3,4,2,0,1:T(8,128)(2,1)} %slice_bitcast_fusion.10), channel_id=1, source_target_pairs={{8,0},{16,8},{24,16},{9,1},{17,9},{25,17},{10,2},{18,10},{26,18},{... | collective-permute-start | bytes 6291464 | tf_op jit(solution)/shard_map/ppermute | solution.py:21
  158.8 98.9 %all-to-all-start.1 = ((bf16[8,1,4,256,256]{3,4,2,1,0:T(8,128)(2,1)}), bf16[8,1,4,256,256]{3,4,2,1,0:T(8,128)(2,1)}, u32[]{:S(2)}, u32[]{:S(2)}) async-start(bf16[8,1,4,256,256]{3,4,2,1,0:T(8,128)(2,1)} %fusion.29), calls=%async_computation.1 | async-start | bytes 8388608 | tf_op jit(solution)/shard_map/all_to_all | solution.py:88
  165.4 63.7 %all-gather.2.cloned.1.call-start = ((), (), s32[]{:S(2)}) async-start(), calls=%async_computation.3 | async-start | bytes 1179648 | tf_op jit(solution)/shard_map/all_gather | solution.py:89
Sparse Core Ops, SparseCore 0:
  168.4 60.7 all-gather.1
where the time goes:
time: 416 us; the launch traced here: 411 us
  blocking collectives  194 us (47%)
  waiting for transfers between devices  102 us (25%)
  matrix products  30.9 us (7%)
  local copies, waits for them, and re-layouts  27.1 us (7%)
  between operations  26.3 us (6%)
  other arithmetic  16.7 us (4%)
  starting transfers between devices  12.6 us (3%)
    all_to_all x1, blocking collectives, body(): lax.all_to_all(finished, 'layer', split_axis=1, concat_axis=0, tiled=True)  97.8 us
    all_to_all x1, blocking collectives, body(): lax.all_to_all(correlations, 'layer', split_axis=1, concat_axis=0, tiled=...  96.5 us
    all_gather x1, waiting for transfers between devices, body(): couplings = lax.all_gather(coupling, 'layer', axis=0, tiled=True)  61.9 us
    all_to_all x1, waiting for transfers between devices, body(): lax.all_to_all(sigma_blocks, 'layer', split_axis=0, concat_axis=1, tiled=...  28.6 us
    dot_general x8, matrix products, advance(): jnp.einsum('ab,...kbc->...kac', coupling_block, halfway, preferred_elemen...  13.7 us
    convert_element_type x1, other arithmetic, body(): sigma_blocks = jnp.where(live_mask, accumulated, 0.0).astype(jnp.bfloat16)  11.6 us
    dot_general x32, matrix products, right_product(): jnp.einsum('...kab,...cb->...kac', stacked_block, matrix, preferred_eleme...  8.78 us
    unnamed x8, local copies, waits for them, and re-layouts  8.45 us
  transfers between devices with their start and end apart: 4, of which 4 were waited for; matrix products, arithmetic and copies ran while one was open for 1% of the time, Pallas kernels for 0%

commit v1 on v0

v1 whole, which is shorter than its diff:
```python
import functools

import jax
import jax.numpy as jnp
from jax import lax
from jax.experimental import pallas as pl
from jax.experimental.pallas import tpu as pltpu
from jax.sharding import PartitionSpec as P

SHIFT_MAX = 4
MESH = pl.DeviceIdType.MESH
ROWS = 32

bose_ratio = 0.5


def tap_weights(phonon_shifts, phonon_coupling):
    occupation = 1.0 / (jnp.exp(bose_ratio * phonon_shifts.astype(jnp.float32)) - 1.0)
    distance = jnp.arange(1, SHIFT_MAX + 1, dtype=jnp.int32)
    here = phonon_shifts[None, :] == distance[:, None]
    absorb = jnp.sum(jnp.where(here, phonon_coupling * occupation, 0.0), axis=1)
    emit = jnp.sum(jnp.where(here, phonon_coupling * (occupation + 1.0), 0.0), axis=1)
    return jnp.concatenate([absorb, emit])


def dot(a, b):
    return lax.dot_general(a, b, (((1,), (0,)), ((), ())), preferred_element_type=jnp.float32)


def dot_t(a, b):
    return lax.dot_general(a, b, (((1,), (1,)), ((), ())), preferred_element_type=jnp.float32)


def kernel(
    groups, lines, orbitals,
    weights, corr, ret, coupling, live, out,
    buf, green, volt, alive, sigma, xin, xout,
    own_sem, line_s, line_r, part_s, part_r, halo_s, halo_r,
    ret_own, ret_s, ret_r, side_sem, chain_s, chain_r, out_sem, out_s, out_r,
):
    energies = 2 * lines
    e = lax.axis_index("energy")
    index = lax.axis_index("layer")
    p = index // 2
    q = lax.rem(index, 2)
    partner = {"layer": 2 * p + (1 - q)}
    half = jnp.bfloat16

    def peer(d):
        return lax.rem(p + d, lines)

    def source(d):
        return lax.rem(p + lines - d, lines)

    barrier = pltpu.get_barrier_semaphore()
    for d in range(1, lines):
        pl.semaphore_signal(barrier, inc=1, device_id={"layer": 2 * peer(d) + q}, device_id_type=MESH)
    pl.semaphore_signal(barrier, inc=1, device_id=partner, device_id_type=MESH)

    @pl.when(e > 0)
    def _():
        pl.semaphore_signal(barrier, inc=1, device_id={"energy": e - 1}, device_id_type=MESH)

    @pl.when(e < groups - 1)
    def _():
        pl.semaphore_signal(barrier, inc=1, device_id={"energy": e + 1}, device_id_type=MESH)

    beside = (e > 0).astype(jnp.int32) + (e < groups - 1).astype(jnp.int32)
    pl.semaphore_wait(barrier, lines + beside)

    def slot_of(line, parity):
        return SHIFT_MAX + 2 * line + parity

    def own_copy(k):
        c, a = divmod(k, 2)
        return pltpu.make_async_copy(
            corr.at[0, 2 * p + a, pl.ds(2 * c, 2)], buf.at[k, slot_of(p, q)], own_sem.at[k]
        )

    def line_copy(k, d, arriving=False):
        c, a = divmod(k, 2)
        line = source(d) if arriving else p
        return pltpu.make_async_remote_copy(
            src_ref=corr.at[0, 2 * peer(d) + a, pl.ds(2 * c, 2)],
            dst_ref=buf.at[k, slot_of(line, q)],
            send_sem=line_s.at[k, d], recv_sem=line_r.at[k, d],
            device_id={"layer": 2 * peer(d) + q}, device_id_type=MESH,
        )

    def part_copy(k, d, arriving=False):
        slot = slot_of(source(d), 1 - q if arriving else q)
        return pltpu.make_async_remote_copy(
            src_ref=buf.at[k, slot], dst_ref=buf.at[k, slot],
            send_sem=part_s.at[k, d], recv_sem=part_r.at[k, d],
            device_id=partner, device_id_type=MESH,
        )

    def halo_copy(k, side):
        first = SHIFT_MAX if side == 0 else energies
        landing = SHIFT_MAX + energies if side == 0 else 0
        return pltpu.make_async_remote_copy(
            src_ref=buf.at[k, pl.ds(first, SHIFT_MAX)],
            dst_ref=buf.at[k, pl.ds(landing, SHIFT_MAX)],
            send_sem=halo_s.at[k, side], recv_sem=halo_r.at[k, side],
            device_id={"energy": e - 1 if side == 0 else e + 1}, device_id_type=MESH,
        )

    def ret_own_copy():
        return pltpu.make_async_copy(ret.at[0, pl.ds(2 * p, 2)], green.at[p], ret_own)

    def ret_copy(d, arriving=False):
        line = source(d) if arriving else p
        return pltpu.make_async_remote_copy(
            src_ref=ret.at[0, pl.ds(2 * peer(d), 2)], dst_ref=green.at[line],
            send_sem=ret_s.at[d], recv_sem=ret_r.at[d],
            device_id={"layer": 2 * peer(d) + q}, device_id_type=MESH,
        )

    def side_copies(arriving=False):
        at = 1 - q if arriving else q
        return (
            pltpu.make_async_remote_copy(
                src_ref=coupling.at[0], dst_ref=volt.at[at],
                send_sem=side_sem.at[0], recv_sem=side_sem.at[1],
                device_id=partner, device_id_type=MESH,
            ),
            pltpu.make_async_remote_copy(
                src_ref=live, dst_ref=alive.at[at],
                send_sem=side_sem.at[2], recv_sem=side_sem.at[3],
                device_id=partner, device_id_type=MESH,
            ),
        )

    def side_own():
        return (
            pltpu.make_async_copy(coupling.at[0], volt.at[q], side_sem.at[4]),
            pltpu.make_async_copy(live, alive.at[q], side_sem.at[5]),
        )

    def chain_copy(c, i):
        return pltpu.make_async_remote_copy(
            src_ref=xout.at[c, 1, i], dst_ref=xin.at[c, i],
            send_sem=chain_s.at[c, i], recv_sem=chain_r.at[c, i],
            device_id={"layer": lax.rem(index + 2, 2 * lines)}, device_id_type=MESH,
        )

    def out_own(c, i):
        return pltpu.make_async_copy(
            xout.at[c, q, i], out.at[2 * i + q, 0, pl.ds(2 * c, 2)], out_sem.at[c, i]
        )

    def out_copy(c, i, arriving=False):
        parity = 1 - q if arriving else q
        return pltpu.make_async_remote_copy(
            src_ref=xout.at[c, 1 - q, i], dst_ref=out.at[2 * i + parity, 0, pl.ds(2 * c, 2)],
            send_sem=out_s.at[c, i], recv_sem=out_r.at[c, i],
            device_id=partner, device_id_type=MESH,
        )

    def start_line(k):
        own_copy(k).start()
        for d in range(1, lines):
            line_copy(k, d).start()

    def pass_on(k):
        for d in range(lines):
            if d == 0:
                own_copy(k).wait()
            else:
                line_copy(k, d, True).wait_recv()
            part_copy(k, d).start()

    def start_halo(k):
        for d in range(lines):
            part_copy(k, d, True).wait_recv()

        @pl.when(e > 0)
        def _():
            halo_copy(k, 0).start()

        @pl.when(e < groups - 1)
        def _():
            halo_copy(k, 1).start()

    def self_energy(k):
        c, a = divmod(k, 2)

        @pl.when(e < groups - 1)
        def _():
            halo_copy(k, 0).wait_recv()

        @pl.when(e > 0)
        def _():
            halo_copy(k, 1).wait_recv()

        absorb = [weights[d] for d in range(SHIFT_MAX)]
        emit = [weights[SHIFT_MAX + d] for d in range(SHIFT_MAX)]
        below, above = (absorb, emit) if c == 0 else (emit, absorb)
        count = alive[a, 0:1, :]
        column = lax.broadcasted_iota(jnp.int32, (ROWS, orbitals), 1)
        row = lax.broadcasted_iota(jnp.int32, (ROWS, orbitals), 0)
        tiles = orbitals // ROWS

        def one(step, carry):
            i = step // (2 * tiles)
            component = lax.rem(step // tiles, 2)
            base = pl.multiple_of(lax.rem(step, tiles) * ROWS, ROWS)
            here = slot_of(i, q)
            total = jnp.zeros((ROWS, orbitals), jnp.float32)
            for d in range(SHIFT_MAX):
                low = buf[k, here - d - 1, component, pl.ds(base, ROWS), :].astype(jnp.float32)
                high = buf[k, here + d + 1, component, pl.ds(base, ROWS), :].astype(jnp.float32)
                total = total + (below[d] * low + above[d] * high)
            keep = (row + base < count) & (column < count)
            sigma[k, i, component, pl.ds(base, ROWS), :] = jnp.where(keep, total, 0.0).astype(half)
            return carry

        lax.fori_loop(0, lines * 2 * tiles, one, 0)

    def advance(c, a, i, previous):
        k = 2 * c + a
        v = volt[a]
        g_real = green[i, a, 0]
        g_imag = green[i, a, 1]
        halfway = [dot_t(previous[n], v).astype(half) for n in range(2)]
        src = [
            (sigma[k, i, n].astype(jnp.float32) + dot(v, halfway[n])).astype(half) for n in range(2)
        ]
        inner_real = (dot(g_real, src[0]) - dot(g_imag, src[1])).astype(half)
        inner_imag = (dot(g_real, src[1]) + dot(g_imag, src[0])).astype(half)
        xout[c, a, i, 0] = (dot_t(inner_real, g_real) + dot_t(inner_imag, g_imag)).astype(half)
        xout[c, a, i, 1] = (dot_t(inner_imag, g_real) - dot_t(inner_real, g_imag)).astype(half)

    def sweep(c, first, last):
        def one(i, carry):
            @pl.when(p == 0)
            def _():
                xin[c, i] = buf[2 * c, slot_of(i, q)]

            @pl.when(p > 0)
            def _():
                chain_copy(c, i).wait_recv()

            advance(c, 0, i, xin.at[c, i])
            advance(c, 1, i, xout.at[c, 0, i])

            @pl.when(p < lines - 1)
            def _():
                chain_copy(c, i).start()

            out_copy(c, i).start()
            out_own(c, i).start()
            return carry

        lax.fori_loop(first, last, one, 0)

    start_line(0)
    for copy in side_own() + side_copies():
        copy.start()
    start_line(1)

    for at, edge in ((0, 0), (SHIFT_MAX + energies, groups - 1)):
        @pl.when(e == edge)
        def _(at=at):
            def clear(step, carry):
                k = step // SHIFT_MAX
                slot = at + lax.rem(step, SHIFT_MAX)
                buf[k, slot] = jnp.zeros(buf.shape[2:], half)
                return carry

            lax.fori_loop(0, 4 * SHIFT_MAX, clear, 0)

    pass_on(0)
    ret_own_copy().start()
    for d in range(1, lines):
        ret_copy(d).start()
    pass_on(1)
    start_line(2)
    start_halo(0)
    start_halo(1)
    for copy in side_own():
        copy.wait()
    for copy in side_copies(True):
        copy.wait_recv()
    self_energy(0)
    self_energy(1)
    ret_own_copy().wait()
    for d in range(1, lines):
        ret_copy(d, True).wait_recv()
    start_line(3)
    middle = lines // 2
    sweep(0, 0, middle)
    pass_on(2)
    sweep(0, middle, lines)
    start_halo(2)
    pass_on(3)
    self_energy(2)
    start_halo(3)
    self_energy(3)
    sweep(1, 0, lines)

    for copy in side_copies():
        copy.wait_send()
    for d in range(1, lines):
        ret_copy(d).wait_send()
        for k in range(4):
            line_copy(k, d).wait_send()
    for k in range(4):
        for d in range(lines):
            part_copy(k, d).wait_send()

        @pl.when(e > 0)
        def _(k=k):
            halo_copy(k, 0).wait_send()

        @pl.when(e < groups - 1)
        def _(k=k):
            halo_copy(k, 1).wait_send()

    for c in range(2):
        def finish(i, carry, c=c):
            @pl.when(p < lines - 1)
            def _():
                chain_copy(c, i).wait_send()

            out_own(c, i).wait()
            out_copy(c, i).wait_send()
            out_copy(c, i, True).wait_recv()
            return carry

        lax.fori_loop(0, lines, finish, 0)


def body(correlations, retarded, coupling, phonon_shifts, phonon_coupling, layer_orbitals):
    groups = lax.axis_size("energy")
    energies = lax.axis_size("layer")
    lines = energies // 2
    orbitals = correlations.shape[-1]
    weights = tap_weights(phonon_shifts, phonon_coupling)
    live = jnp.broadcast_to(layer_orbitals[0], (8, orbitals)).astype(jnp.int32)
    block = (2, orbitals, orbitals)
    low = jnp.bfloat16
    shapes = [
        (4, energies + 2 * SHIFT_MAX) + block,
        (lines, 2) + block,
        (2, orbitals, orbitals),
        None,
        (4, lines) + block,
        (2, lines) + block,
        (2, 2, lines) + block,
    ]
    scratch = [
        pltpu.VMEM((2, 8, orbitals), jnp.int32) if shape is None else pltpu.VMEM(shape, low)
        for shape in shapes
    ]
    blocks = 4 * (energies + 2 * SHIFT_MAX) + 2 * lines + 1 + 4 * lines + 2 * lines + 4 * lines
    dma = pltpu.SemaphoreType.DMA
    semaphores = [
        dma((4,)), dma((4, lines)), dma((4, lines)), dma((4, lines)), dma((4, lines)),
        dma((4, 2)), dma((4, 2)),
        dma(()), dma((lines,)), dma((lines,)), dma((6,)),
        dma((2, lines)), dma((2, lines)), dma((2, lines)), dma((2, lines)), dma((2, lines)),
    ]
    anywhere = pl.BlockSpec(memory_space=pl.ANY)
    return pl.pallas_call(
        functools.partial(kernel, groups, lines, orbitals),
        out_shape=jax.ShapeDtypeStruct((energies, 1, 4, orbitals, orbitals), low),
        in_specs=[pl.BlockSpec(memory_space=pltpu.SMEM)] + [anywhere] * 4,
        out_specs=anywhere,
        scratch_shapes=scratch + semaphores,
        compiler_params=pltpu.CompilerParams(
            collective_id=0, has_side_effects=True,
            vmem_limit_bytes=blocks * 4 * orbitals * orbitals + (8 << 20),
        ),
        cost_estimate=pl.CostEstimate(
            flops=lines * 4 * 12 * 2 * orbitals**3, bytes_accessed=12 << 20, transcendentals=0
        ),
    )(weights, correlations, retarded, coupling, live)


def solution(mesh):
    return jax.shard_map(
        body,
        mesh=mesh,
        in_specs=(
            P(("energy", "layer"), None, None, None, None),
            P(("energy", "layer"), None, None, None, None),
            P("layer", None, None),
            P(),
            P(),
            P("layer"),
        ),
        out_specs=P("energy", "layer", None, None, None),
        check_vma=False,
    )
```

time: 416 us -> 267 us (0.64)
  Pallas kernels: 0 us -> 255 us
  blocking collectives: 194 us -> 0 us
  waiting for transfers between devices: 102 us -> 0 us
  matrix products: 30.9 us -> 0 us
  between operations: 26.3 us -> 0.67 us
  local copies, waits for them, and re-layouts: 27.1 us -> 6.71 us
  other arithmetic: 16.7 us -> 2.3 us
  starting transfers between devices: 12.6 us -> 0 us
    pallas_call x0 -> x1, Pallas kernels: none -> 255 us  [body(): pl.pallas_call(functools.partial(kernel, groups, lines, orbitals), out_sh...]
    all_to_all x2 -> x0, blocking collectives: 194 us -> none  [the longest x1 97.8 us: body(): lax.all_to_all(finished, 'layer', split_axis=1, concat_axis=0, tiled=True)]
    all_gather x1 -> x0, waiting for transfers between devices: 61.9 us -> none  [body(): couplings = lax.all_gather(coupling, 'layer', axis=0, tiled=True)]
    dot_general x72 -> x0, matrix products: 30.9 us -> none  [the longest x8 13.7 us: advance(): jnp.einsum('ab,...kbc->...kac', coupling_block, halfway, preferred_elemen...]
    all_to_all x1 -> x0, waiting for transfers between devices: 28.6 us -> none  [body(): lax.all_to_all(sigma_blocks, 'layer', split_axis=0, concat_axis=1, tiled=...]
    convert_element_type x9 -> x0, other arithmetic: 12 us -> none  [the longest x1 11.6 us: body(): sigma_blocks = jnp.where(live_mask, accumulated, 0.0).astype(jnp.bfloat16)]
    ppermute x2 -> x0, waiting for transfers between devices: 11.2 us -> none  [the longest x1 6.21 us: with_halo(): lax.ppermute(lax.slice_in_dim(block, 0, width, axis=dim), axis, backward)]
    squeeze x9 -> x0, local copies, waits for them, and re-layouts: 8.81 us -> none  [the longest x8 7.74 us: layer_step(): lax.dynamic_index_in_dim(retarded, layer_index, 1, keepdims=False)]
  transfers between devices with their start and end apart: 4 -> 0, of which waited for: 4 -> 0; matrix products, arithmetic and copies ran while one was open for 1% -> 0% of each run, Pallas kernels for 0% -> 0%
where the time goes in v1:
time: 267 us; the launch traced here: 265 us
  Pallas kernels  255 us (96%)
  local copies, waits for them, and re-layouts  6.71 us (3%)
    pallas_call x1, Pallas kernels, body(): pl.pallas_call(functools.partial(kernel, groups, lines, orbitals), out_sh...  255 us
    unnamed x7, local copies, waits for them, and re-layouts  6.71 us

profile of v1, /device:TPU:27, one launch (start us, length us, event | category | flops | bytes accessed | tf_op | source)
XLA Modules:
  0.0 265.0 jit_solution(12644159295897983455)
XLA Ops:
  0.7 0.7 add_multiply_fusion
  1.3 0.7 mul.10
  2.0 0.9 fusion
  2.9 0.1 pad_maximum_fusion.weights
  3.0 0.0 copy-start
  3.0 2.2 copy-done
  5.2 0.0 copy-start.1
  5.2 1.6 copy-done.1
  6.7 0.0 copy-start.2
  6.8 0.9 copy-done.2
  7.7 255.3 %shard_map.64 = bf16[8,1,4,256,256]{4,3,2,1,0:T(8,128)(2,1)S(1)} custom-call(f32[8]{0:T(128)S(1)} %pad_maximum_fusion.weights, bf16[1,8,4,256,256]{4,3,2,1,0:T(8,128)(2,1)S(1)} %copy-done, bf16[1,8,2,256,256]{4,3,2,1,0:T(8,128)(2,1)S(1)} %copy-done.1, bf16[1,256,256]{2,1,0:T(8,128)(2,1)S(1)} %copy-done.2, s32[8,256]{1,0:T(8,128)S(1)} %broadcast_in_dim.20.live), custom_call_target="tpu_custom_call" | custom-call | flops 6442450944 | bytes 12582912 | tf_op jit(solution)/shard_map/pallas_call | solution.py:365
  263.0 2.0 copy.9
  (2 shorter events, 0.0 us)
Async XLA Ops:
  3.0 2.2 copy-start
  5.2 1.6 copy-start.1
  6.7 0.9 copy-start.2

commit v2 on v1

--- a/solution.py
+++ b/solution.py
@@ -1,4 +1,5 @@
 import functools
+import math
 
 import jax
 import jax.numpy as jnp
@@ -14,13 +15,16 @@
 bose_ratio = 0.5
 
 
-def tap_weights(phonon_shifts, phonon_coupling):
-    occupation = 1.0 / (jnp.exp(bose_ratio * phonon_shifts.astype(jnp.float32)) - 1.0)
-    distance = jnp.arange(1, SHIFT_MAX + 1, dtype=jnp.int32)
-    here = phonon_shifts[None, :] == distance[:, None]
-    absorb = jnp.sum(jnp.where(here, phonon_coupling * occupation, 0.0), axis=1)
-    emit = jnp.sum(jnp.where(here, phonon_coupling * (occupation + 1.0), 0.0), axis=1)
-    return jnp.concatenate([absorb, emit])
+def tap_weights(shifts, strengths):
+    absorb, emit = [], []
+    for distance in range(1, SHIFT_MAX + 1):
+        strength = jnp.float32(0)
+        for mode in range(shifts.shape[0]):
+            strength += jnp.where(shifts[mode] == distance, strengths[mode], jnp.float32(0))
+        occupation = 1.0 / math.expm1(bose_ratio * distance)
+        absorb.append(strength * jnp.float32(occupation))
+        emit.append(strength * jnp.float32(occupation + 1.0))
+    return absorb, emit
 
 
 def dot(a, b):
@@ -33,7 +37,7 @@
 
 def kernel(
     groups, lines, orbitals,
-    weights, corr, ret, coupling, live, out,
+    shifts, strengths, orbital_count, corr, ret, coupling, out,
     buf, green, volt, alive, sigma, xin, xout,
     own_sem, line_s, line_r, part_s, part_r, halo_s, halo_r,
     ret_own, ret_s, ret_r, side_sem, chain_s, chain_r, out_sem, out_s, out_r,
@@ -125,17 +129,14 @@
                 device_id=partner, device_id_type=MESH,
             ),
             pltpu.make_async_remote_copy(
-                src_ref=live, dst_ref=alive.at[at],
+                src_ref=alive.at[at], dst_ref=alive.at[at],
                 send_sem=side_sem.at[2], recv_sem=side_sem.at[3],
                 device_id=partner, device_id_type=MESH,
             ),
         )
 
     def side_own():
-        return (
-            pltpu.make_async_copy(coupling.at[0], volt.at[q], side_sem.at[4]),
-            pltpu.make_async_copy(live, alive.at[q], side_sem.at[5]),
-        )
+        return pltpu.make_async_copy(coupling.at[0], volt.at[q], side_sem.at[4])
 
     def chain_copy(c, i):
         return pltpu.make_async_remote_copy(
@@ -162,13 +163,23 @@
         for d in range(1, lines):
             line_copy(k, d).start()
 
-    def pass_on(k):
-        for d in range(lines):
-            if d == 0:
-                own_copy(k).wait()
-            else:
+    def arrival(t):
+        line = jnp.where(p < lines // 2, t, lines - 1 - t)
+        return line, lax.rem(p + lines - line, lines)
+
+    def pass_on(k, meanwhile=None):
+        own_copy(k).wait()
+        part_copy(k, 0).start()
+        for t in range(lines):
+            line, d = arrival(t)
+
+            @pl.when(line != p)
+            def _():
                 line_copy(k, d, True).wait_recv()
-            part_copy(k, d).start()
+                part_copy(k, d).start()
+
+            if t == lines // 2 and meanwhile is not None:
+                meanwhile()
 
     def start_halo(k):
         for d in range(lines):
@@ -193,8 +204,7 @@
         def _():
             halo_copy(k, 1).wait_recv()
 
-        absorb = [weights[d] for d in range(SHIFT_MAX)]
-        emit = [weights[SHIFT_MAX + d] for d in range(SHIFT_MAX)]
+        absorb, emit = tap_weights(shifts, strengths)
         below, above = (absorb, emit) if c == 0 else (emit, absorb)
         count = alive[a, 0:1, :]
         column = lax.broadcasted_iota(jnp.int32, (ROWS, orbitals), 1)
@@ -246,6 +256,10 @@
 
             @pl.when(p < lines - 1)
             def _():
+                @pl.when(i > 0)
+                def _():
+                    chain_copy(c, i - 1).wait_send()
+
                 chain_copy(c, i).start()
 
             out_copy(c, i).start()
@@ -255,9 +269,10 @@
         lax.fori_loop(first, last, one, 0)
 
     start_line(0)
-    for copy in side_own() + side_copies():
+    alive[q] = jnp.full(alive.shape[1:], orbital_count[0], jnp.int32)
+    side_own().start()
+    for copy in side_copies():
         copy.start()
-    start_line(1)
 
     for at, edge in ((0, 0), (SHIFT_MAX + energies, groups - 1)):
         @pl.when(e == edge)
@@ -270,16 +285,17 @@
 
             lax.fori_loop(0, 4 * SHIFT_MAX, clear, 0)
 
-    pass_on(0)
-    ret_own_copy().start()
-    for d in range(1, lines):
-        ret_copy(d).start()
-    pass_on(1)
+    def start_ret():
+        ret_own_copy().start()
+        for d in range(1, lines):
+            ret_copy(d).start()
+
+    pass_on(0, lambda: start_line(1))
+    pass_on(1, start_ret)
+    start_halo(0)
     start_line(2)
-    start_halo(0)
     start_halo(1)
-    for copy in side_own():
-        copy.wait()
+    side_own().wait()
     for copy in side_copies(True):
         copy.wait_recv()
     self_energy(0)
@@ -288,10 +304,8 @@
     for d in range(1, lines):
         ret_copy(d, True).wait_recv()
     start_line(3)
-    middle = lines // 2
-    sweep(0, 0, middle)
+    sweep(0, 0, lines)
     pass_on(2)
-    sweep(0, middle, lines)
     start_halo(2)
     pass_on(3)
     self_energy(2)
@@ -319,7 +333,7 @@
 
     for c in range(2):
         def finish(i, carry, c=c):
-            @pl.when(p < lines - 1)
+            @pl.when((p < lines - 1) & (i == lines - 1))
             def _():
                 chain_copy(c, i).wait_send()
 
@@ -336,8 +350,6 @@
     energies = lax.axis_size("layer")
     lines = energies // 2
     orbitals = correlations.shape[-1]
-    weights = tap_weights(phonon_shifts, phonon_coupling)
-    live = jnp.broadcast_to(layer_orbitals[0], (8, orbitals)).astype(jnp.int32)
     block = (2, orbitals, orbitals)
     low = jnp.bfloat16
     shapes = [
@@ -353,7 +365,6 @@
         pltpu.VMEM((2, 8, orbitals), jnp.int32) if shape is None else pltpu.VMEM(shape, low)
         for shape in shapes
     ]
-    blocks = 4 * (energies + 2 * SHIFT_MAX) + 2 * lines + 1 + 4 * lines + 2 * lines + 4 * lines
     dma = pltpu.SemaphoreType.DMA
     semaphores = [
         dma((4,)), dma((4, lines)), dma((4, lines)), dma((4, lines)), dma((4, lines)),
@@ -365,17 +376,17 @@
     return pl.pallas_call(
         functools.partial(kernel, groups, lines, orbitals),
         out_shape=jax.ShapeDtypeStruct((energies, 1, 4, orbitals, orbitals), low),
-        in_specs=[pl.BlockSpec(memory_space=pltpu.SMEM)] + [anywhere] * 4,
+        in_specs=[pl.BlockSpec(memory_space=pltpu.SMEM)] * 3 + [anywhere] * 3,
         out_specs=anywhere,
         scratch_shapes=scratch + semaphores,
         compiler_params=pltpu.CompilerParams(
             collective_id=0, has_side_effects=True,
-            vmem_limit_bytes=blocks * 4 * orbitals * orbitals + (8 << 20),
+            vmem_limit_bytes=60 << 20,
         ),
         cost_estimate=pl.CostEstimate(
             flops=lines * 4 * 12 * 2 * orbitals**3, bytes_accessed=12 << 20, transcendentals=0
         ),
-    )(weights, correlations, retarded, coupling, live)
+    )(phonon_shifts, phonon_coupling, layer_orbitals, correlations, retarded, coupling)
 
 
 def solution(mesh):

time: 267 us -> 266 us (level)
  Pallas kernels: 255 us -> 261 us
    pallas_call x1, Pallas kernels: 255 us -> 261 us  [body(): pl.pallas_call(functools.partial(kernel, groups, lines, orbitals), out_sh...]
    unnamed x7 -> x1, local copies, waits for them, and re-layouts: 6.71 us -> 4.64 us
where the time goes in v2:
time: 266 us
  Pallas kernels  261 us (98%)
  local copies, waits for them, and re-layouts  4.64 us (2%)
    pallas_call x1, Pallas kernels, body(): pl.pallas_call(functools.partial(kernel, groups, lines, orbitals), out_sh...  261 us

profile of v2, /device:TPU:27, one launch (start us, length us, event | category | flops | bytes accessed | tf_op | source)
XLA Modules:
  0.0 265.9 jit_solution(5058698321714958269)
XLA Ops:
  0.7 260.6 %shard_map.64 = bf16[8,1,4,256,256]{4,3,2,1,0:T(8,128)(2,1)} custom-call(s32[4]{0:T(128)} %shifts.1, f32[4]{0:T(128)} %strengths.1, s32[1]{0:T(128)S(6)} %copy.8.orbital_count, bf16[1,8,4,256,256]{4,3,2,1,0:T(8,128)(2,1)} %corr.1, bf16[1,8,2,256,256]{4,3,2,1,0:T(8,128)(2,1)} %ret.1, bf16[1,256,256]{2,1,0:T(8,128)(2,1)} %coupling.1), custom_call_target="tpu_custom_call" | custom-call | flops 6442450944 | bytes 12582912 | tf_op jit(solution)/shard_map/pallas_call | solution.py:376
  261.3 4.6 %copy.9 = bf16[8,1,4,256,256]{4,3,2,1,0:T(8,128)(2,1)} copy(bf16[8,1,4,256,256]{4,3,2,1,0:T(8,128)(2,1)} %shard_map.64) | data formatting | bytes 8388608

commit v3 on v2

--- a/solution.py
+++ b/solution.py
@@ -167,7 +167,7 @@
         line = jnp.where(p < lines // 2, t, lines - 1 - t)
         return line, lax.rem(p + lines - line, lines)
 
-    def pass_on(k, meanwhile=None):
+    def pass_on(k):
         own_copy(k).wait()
         part_copy(k, 0).start()
         for t in range(lines):
@@ -177,9 +177,6 @@
             def _():
                 line_copy(k, d, True).wait_recv()
                 part_copy(k, d).start()
-
-            if t == lines // 2 and meanwhile is not None:
-                meanwhile()
 
     def start_halo(k):
         for d in range(lines):
@@ -241,35 +238,45 @@
         xout[c, a, i, 0] = (dot_t(inner_real, g_real) + dot_t(inner_imag, g_imag)).astype(half)
         xout[c, a, i, 1] = (dot_t(inner_imag, g_real) - dot_t(inner_real, g_imag)).astype(half)
 
-    def sweep(c, first, last):
-        def one(i, carry):
+    def sweep_energy(i, carry):
+        @pl.when(i == p)
+        def _():
+            ret_own_copy().wait()
+
+        @pl.when(i != p)
+        def _():
+            ret_copy(lax.rem(p + lines - i, lines), True).wait_recv()
+
+        for c in range(2):
             @pl.when(p == 0)
-            def _():
+            def _(c=c):
                 xin[c, i] = buf[2 * c, slot_of(i, q)]
 
             @pl.when(p > 0)
-            def _():
+            def _(c=c):
                 chain_copy(c, i).wait_recv()
 
             advance(c, 0, i, xin.at[c, i])
             advance(c, 1, i, xout.at[c, 0, i])
 
             @pl.when(p < lines - 1)
-            def _():
-                @pl.when(i > 0)
-                def _():
-                    chain_copy(c, i - 1).wait_send()
+            def _(c=c):
+                if c == 1:
+                    chain_copy(0, i).wait_send()
+                else:
+                    @pl.when(i > 0)
+                    def _():
+                        chain_copy(1, i - 1).wait_send()
 
                 chain_copy(c, i).start()
 
             out_copy(c, i).start()
             out_own(c, i).start()
-            return carry
-
-        lax.fori_loop(first, last, one, 0)
+        return carry
 
     start_line(0)
     alive[q] = jnp.full(alive.shape[1:], orbital_count[0], jnp.int32)
+    start_line(1)
     side_own().start()
     for copy in side_copies():
         copy.start()
@@ -290,28 +297,25 @@
         for d in range(1, lines):
             ret_copy(d).start()
 
-    pass_on(0, lambda: start_line(1))
-    pass_on(1, start_ret)
+    pass_on(0)
+    start_line(2)
+    pass_on(1)
+    start_line(3)
     start_halo(0)
-    start_line(2)
+    pass_on(2)
+    start_ret()
     start_halo(1)
     side_own().wait()
     for copy in side_copies(True):
         copy.wait_recv()
     self_energy(0)
+    pass_on(3)
+    start_halo(2)
     self_energy(1)
-    ret_own_copy().wait()
-    for d in range(1, lines):
-        ret_copy(d, True).wait_recv()
-    start_line(3)
-    sweep(0, 0, lines)
-    pass_on(2)
-    start_halo(2)
-    pass_on(3)
+    start_halo(3)
     self_energy(2)
-    start_halo(3)
     self_energy(3)
-    sweep(1, 0, lines)
+    lax.fori_loop(0, lines, sweep_energy, 0)
 
     for copy in side_copies():
         copy.wait_send()
@@ -331,12 +335,12 @@
         def _(k=k):
             halo_copy(k, 1).wait_send()
 
+    @pl.when(p < lines - 1)
+    def _():
+        chain_copy(1, lines - 1).wait_send()
+
     for c in range(2):
         def finish(i, carry, c=c):
-            @pl.when((p < lines - 1) & (i == lines - 1))
-            def _():
-                chain_copy(c, i).wait_send()
-
             out_own(c, i).wait()
             out_copy(c, i).wait_send()
             out_copy(c, i, True).wait_recv()
@@ -365,6 +369,7 @@
         pltpu.VMEM((2, 8, orbitals), jnp.int32) if shape is None else pltpu.VMEM(shape, low)
         for shape in shapes
     ]
+    blocks = 4 * (energies + 2 * SHIFT_MAX) + 12 * lines + 1
     dma = pltpu.SemaphoreType.DMA
     semaphores = [
         dma((4,)), dma((4, lines)), dma((4, lines)), dma((4, lines)), dma((4, lines)),
@@ -372,16 +377,17 @@
         dma(()), dma((lines,)), dma((lines,)), dma((6,)),
         dma((2, lines)), dma((2, lines)), dma((2, lines)), dma((2, lines)), dma((2, lines)),
     ]
+    large = pl.BlockSpec(memory_space=pltpu.HBM)
     anywhere = pl.BlockSpec(memory_space=pl.ANY)
     return pl.pallas_call(
         functools.partial(kernel, groups, lines, orbitals),
         out_shape=jax.ShapeDtypeStruct((energies, 1, 4, orbitals, orbitals), low),
-        in_specs=[pl.BlockSpec(memory_space=pltpu.SMEM)] * 3 + [anywhere] * 3,
+        in_specs=[pl.BlockSpec(memory_space=pltpu.SMEM)] * 3 + [large] * 3,
         out_specs=anywhere,
         scratch_shapes=scratch + semaphores,
         compiler_params=pltpu.CompilerParams(
             collective_id=0, has_side_effects=True,
-            vmem_limit_bytes=60 << 20,
+            vmem_limit_bytes=blocks * 4 * orbitals * orbitals + (6 << 20),
         ),
         cost_estimate=pl.CostEstimate(
             flops=lines * 4 * 12 * 2 * orbitals**3, bytes_accessed=12 << 20, transcendentals=0

time: 266 us -> 219 us (0.82)
  Pallas kernels: 261 us -> 210 us
  local copies, waits for them, and re-layouts: 4.64 us -> 8 us
    pallas_call x1, Pallas kernels: 261 us -> 210 us  [body(): pl.pallas_call(functools.partial(kernel, groups, lines, orbitals), out_sh...]
    unnamed x1 -> x11, local copies, waits for them, and re-layouts: 4.64 us -> 8 us
where the time goes in v3:
time: 219 us
  Pallas kernels  210 us (96%)
  local copies, waits for them, and re-layouts  8 us (4%)
    pallas_call x1, Pallas kernels, body(): pl.pallas_call(functools.partial(kernel, groups, lines, orbitals), out_sh...  210 us
    unnamed x11, local copies, waits for them, and re-layouts  8 us

profile of v3, /device:TPU:27, one launch (start us, length us, event | category | flops | bytes accessed | tf_op | source)
XLA Modules:
  0.0 219.1 jit_solution(3359054512817044051)
XLA Ops:
  0.7 0.0 copy-start
  0.7 2.2 copy-done
  2.8 0.0 copy-start.1
  2.8 1.6 copy-done.1
  4.4 0.0 copy-start.2
  4.4 0.9 copy-done.2
  5.3 0.0 copy-start.3
  5.3 0.7 copy-done.3
  6.0 0.0 copy-start.4
  6.0 0.7 copy-done.4
  6.6 210.4 %shard_map.64 = bf16[8,1,4,256,256]{4,3,2,1,0:T(8,128)(2,1)S(1)} custom-call(s32[4]{0:T(128)S(1)} %copy-done.3, f32[4]{0:T(128)S(1)} %copy-done.4, s32[1]{0:T(128)S(6)} %copy.8.orbital_count, bf16[1,8,4,256,256]{4,3,2,1,0:T(8,128)(2,1)S(1)} %copy-done, bf16[1,8,2,256,256]{4,3,2,1,0:T(8,128)(2,1)S(1)} %copy-done.1, bf16[1,256,256]{2,1,0:T(8,128)(2,1)S(1)} %copy-done.2), custom_call_target="tpu_custom_call" | custom-call | flops 6442450944 | bytes 12582912 | tf_op jit(solution)/shard_map/pallas_call | solution.py:382
  217.1 2.0 copy.9
Async XLA Ops:
  0.7 2.2 copy-start
  2.8 1.6 copy-start.1
  4.4 0.9 copy-start.2
  5.3 0.7 copy-start.3
  6.0 0.7 copy-start.4

commit v4 on v3

--- a/solution.py
+++ b/solution.py
@@ -257,7 +257,16 @@
                 chain_copy(c, i).wait_recv()
 
             advance(c, 0, i, xin.at[c, i])
+
+            @pl.when(q == 1)
+            def _(c=c):
+                out_copy(c, i).start()
+
             advance(c, 1, i, xout.at[c, 0, i])
+
+            @pl.when(q == 0)
+            def _(c=c):
+                out_copy(c, i).start()
 
             @pl.when(p < lines - 1)
             def _(c=c):
@@ -270,13 +279,13 @@
 
                 chain_copy(c, i).start()
 
-            out_copy(c, i).start()
             out_own(c, i).start()
         return carry
 
     start_line(0)
     alive[q] = jnp.full(alive.shape[1:], orbital_count[0], jnp.int32)
     start_line(1)
+    start_line(2)
     side_own().start()
     for copy in side_copies():
         copy.start()
@@ -298,12 +307,11 @@
             ret_copy(d).start()
 
     pass_on(0)
-    start_line(2)
+    start_line(3)
     pass_on(1)
-    start_line(3)
+    start_ret()
     start_halo(0)
     pass_on(2)
-    start_ret()
     start_halo(1)
     side_own().wait()
     for copy in side_copies(True):
@@ -369,7 +377,6 @@
         pltpu.VMEM((2, 8, orbitals), jnp.int32) if shape is None else pltpu.VMEM(shape, low)
         for shape in shapes
     ]
-    blocks = 4 * (energies + 2 * SHIFT_MAX) + 12 * lines + 1
     dma = pltpu.SemaphoreType.DMA
     semaphores = [
         dma((4,)), dma((4, lines)), dma((4, lines)), dma((4, lines)), dma((4, lines)),
@@ -387,7 +394,7 @@
         scratch_shapes=scratch + semaphores,
         compiler_params=pltpu.CompilerParams(
             collective_id=0, has_side_effects=True,
-            vmem_limit_bytes=blocks * 4 * orbitals * orbitals + (6 << 20),
+            vmem_limit_bytes=60 << 20,
         ),
         cost_estimate=pl.CostEstimate(
             flops=lines * 4 * 12 * 2 * orbitals**3, bytes_accessed=12 << 20, transcendentals=0

time: 219 us -> 229 us (1.046)
  Pallas kernels: 210 us -> 224 us
  local copies, waits for them, and re-layouts: 8 us -> 4.64 us
    pallas_call x1, Pallas kernels: 210 us -> 224 us  [body(): pl.pallas_call(functools.partial(kernel, groups, lines, orbitals), out_sh...]
    unnamed x11 -> x1, local copies, waits for them, and re-layouts: 8 us -> 4.64 us
where the time goes in v4:
time: 229 us
  Pallas kernels  224 us (98%)
  local copies, waits for them, and re-layouts  4.64 us (2%)
    pallas_call x1, Pallas kernels, body(): pl.pallas_call(functools.partial(kernel, groups, lines, orbitals), out_sh...  224 us
    unnamed x1, local copies, waits for them, and re-layouts  4.64 us

profile of v4, /device:TPU:27, one launch (start us, length us, event | category | flops | bytes accessed | tf_op | source)
XLA Modules:
  0.0 228.8 jit_solution(1432073802235153908)
XLA Ops:
  0.7 223.5 %shard_map.64 = bf16[8,1,4,256,256]{4,3,2,1,0:T(8,128)(2,1)} custom-call(s32[4]{0:T(128)} %shifts.1, f32[4]{0:T(128)} %strengths.1, s32[1]{0:T(128)S(6)} %copy.8.orbital_count, bf16[1,8,4,256,256]{4,3,2,1,0:T(8,128)(2,1)} %corr.1, bf16[1,8,2,256,256]{4,3,2,1,0:T(8,128)(2,1)} %ret.1, bf16[1,256,256]{2,1,0:T(8,128)(2,1)} %coupling.1), custom_call_target="tpu_custom_call" | custom-call | flops 6442450944 | bytes 12582912 | tf_op jit(solution)/shard_map/pallas_call | solution.py:389
  224.2 4.6 %copy.9 = bf16[8,1,4,256,256]{4,3,2,1,0:T(8,128)(2,1)} copy(bf16[8,1,4,256,256]{4,3,2,1,0:T(8,128)(2,1)} %shard_map.64) | data formatting | bytes 8388608

commit v5 on v4

--- a/solution.py
+++ b/solution.py
@@ -377,6 +377,7 @@
         pltpu.VMEM((2, 8, orbitals), jnp.int32) if shape is None else pltpu.VMEM(shape, low)
         for shape in shapes
     ]
+    blocks = 4 * (energies + 2 * SHIFT_MAX) + 12 * lines + 1
     dma = pltpu.SemaphoreType.DMA
     semaphores = [
         dma((4,)), dma((4, lines)), dma((4, lines)), dma((4, lines)), dma((4, lines)),
@@ -394,7 +395,7 @@
         scratch_shapes=scratch + semaphores,
         compiler_params=pltpu.CompilerParams(
             collective_id=0, has_side_effects=True,
-            vmem_limit_bytes=60 << 20,
+            vmem_limit_bytes=blocks * 4 * orbitals * orbitals + (6 << 20),
         ),
         cost_estimate=pl.CostEstimate(
             flops=lines * 4 * 12 * 2 * orbitals**3, bytes_accessed=12 << 20, transcendentals=0

time: 229 us -> 231 us (level)
  local copies, waits for them, and re-layouts: 4.64 us -> 8 us
    unnamed x1 -> x11, local copies, waits for them, and re-layouts: 4.64 us -> 8 us
where the time goes in v5:
time: 231 us
  Pallas kernels  223 us (97%)
  local copies, waits for them, and re-layouts  8 us (3%)
    pallas_call x1, Pallas kernels, body(): pl.pallas_call(functools.partial(kernel, groups, lines, orbitals), out_sh...  223 us
    unnamed x11, local copies, waits for them, and re-layouts  8 us

profile of v5, /device:TPU:27, one launch (start us, length us, event | category | flops | bytes accessed | tf_op | source)
XLA Modules:
  0.0 231.2 jit_solution(18065363588528535524)
XLA Ops:
  0.7 0.0 copy-start
  0.7 2.2 copy-done
  2.8 0.0 copy-start.1
  2.8 1.6 copy-done.1
  4.4 0.0 copy-start.2
  4.4 0.9 copy-done.2
  5.3 0.0 copy-start.3
  5.3 0.7 copy-done.3
  6.0 0.0 copy-start.4
  6.0 0.7 copy-done.4
  6.6 222.5 %shard_map.64 = bf16[8,1,4,256,256]{4,3,2,1,0:T(8,128)(2,1)S(1)} custom-call(s32[4]{0:T(128)S(1)} %copy-done.3, f32[4]{0:T(128)S(1)} %copy-done.4, s32[1]{0:T(128)S(6)} %copy.8.orbital_count, bf16[1,8,4,256,256]{4,3,2,1,0:T(8,128)(2,1)S(1)} %copy-done, bf16[1,8,2,256,256]{4,3,2,1,0:T(8,128)(2,1)S(1)} %copy-done.1, bf16[1,256,256]{2,1,0:T(8,128)(2,1)S(1)} %copy-done.2), custom_call_target="tpu_custom_call" | custom-call | flops 6442450944 | bytes 12582912 | tf_op jit(solution)/shard_map/pallas_call | solution.py:390
  229.2 2.0 copy.9
Async XLA Ops:
  0.7 2.2 copy-start
  2.8 1.6 copy-start.1
  4.4 0.9 copy-start.2
  5.3 0.7 copy-start.3
  6.0 0.7 copy-start.4

commit v6 on v4

--- a/solution.py
+++ b/solution.py
@@ -285,7 +285,6 @@
     start_line(0)
     alive[q] = jnp.full(alive.shape[1:], orbital_count[0], jnp.int32)
     start_line(1)
-    start_line(2)
     side_own().start()
     for copy in side_copies():
         copy.start()
@@ -307,11 +306,12 @@
             ret_copy(d).start()
 
     pass_on(0)
+    start_line(2)
+    pass_on(1)
     start_line(3)
-    pass_on(1)
-    start_ret()
     start_halo(0)
     pass_on(2)
+    start_ret()
     start_halo(1)
     side_own().wait()
     for copy in side_copies(True):

time: 229 us -> 218 us (0.952)
  Pallas kernels: 224 us -> 212 us
    pallas_call x1, Pallas kernels: 224 us -> 212 us  [body(): pl.pallas_call(functools.partial(kernel, groups, lines, orbitals), out_sh...]
where the time goes in v6:
time: 218 us
  Pallas kernels  212 us (97%)
  local copies, waits for them, and re-layouts  4.64 us (2%)
    pallas_call x1, Pallas kernels, body(): pl.pallas_call(functools.partial(kernel, groups, lines, orbitals), out_sh...  212 us
    unnamed x1, local copies, waits for them, and re-layouts  4.64 us

profile of v6, /device:TPU:27, one launch (start us, length us, event | category | flops | bytes accessed | tf_op | source)
XLA Modules:
  0.0 217.6 jit_solution(5952296303342718482)
XLA Ops:
  0.7 212.3 %shard_map.64 = bf16[8,1,4,256,256]{4,3,2,1,0:T(8,128)(2,1)} custom-call(s32[4]{0:T(128)} %shifts.1, f32[4]{0:T(128)} %strengths.1, s32[1]{0:T(128)S(6)} %copy.8.orbital_count, bf16[1,8,4,256,256]{4,3,2,1,0:T(8,128)(2,1)} %corr.1, bf16[1,8,2,256,256]{4,3,2,1,0:T(8,128)(2,1)} %ret.1, bf16[1,256,256]{2,1,0:T(8,128)(2,1)} %coupling.1), custom_call_target="tpu_custom_call" | custom-call | flops 6442450944 | bytes 12582912 | tf_op jit(solution)/shard_map/pallas_call | solution.py:389
  213.0 4.6 %copy.9 = bf16[8,1,4,256,256]{4,3,2,1,0:T(8,128)(2,1)} copy(bf16[8,1,4,256,256]{4,3,2,1,0:T(8,128)(2,1)} %shard_map.64) | data formatting | bytes 8388608
